TPU v7x, 256 devices: a whole 4x4x8 slice. The times are simulated.
256 devices in a mesh: section: 8 (over z_hi, x), dp: 32 (over z_lo, y, core).
Axes of the slice: x: 4, y: 4, z: 8 (z_hi: 2, z_lo: 4; z = z_hi * 4 + z_lo), core: 2. Of those that a mesh axis runs over, the one named last changes fastest.
Arguments:
- inputs: bfloat16 [32, 128, 8192], P(None, 'dp'), may hold values from -16 to 16
- layer_gain: float32 [8, 8192], P('section'), may hold values from 0.5 to 1.5
- layer_down: bfloat16 [8, 8192, 128], P('section', 'dp'), may hold values from -0.0625 to 0.0625
- layer_up: bfloat16 [8, 128, 8192], P('section', None, 'dp'), may hold values from -0.5 to 0.5
- exit_norm_gain: float32 [8192], replicated, may hold values from 0.5 to 1.5
- head_weight: bfloat16 [8192, 16384], P('section', 'dp'), may hold values from -0.1875 to 0.1875
- targets: int32 [32, 128], replicated, may hold values from 0 to 16383
- exit_section: int32 [32], replicated, may hold values from 0 to 7, as said below
Outputs:
- exit_loss: float32 [8, 4, 128], P('section', None, 'dp')
Inputs may be any that keep to these rules, and one draw needn't show every extreme that they name: `exit_section`: each of the 8 sections is the exit of exactly 4 micro-batches.
All inputs are finite; a program needn't handle non-finite values.
Results may differ from a plain program's by a relative error of at most 0.0044.
Values may be sent and summed in bfloat16 or wider, within the bound.
No kernel may reach another device: no remote copies, remote signals or barrier semaphores. Data moves between devices by JAX's collectives and lax.ppermute only.
A program may use at most 128 MiB of HBM per device.

v0:
```python
import jax
import jax.numpy as jnp
from jax import lax
from jax.sharding import PartitionSpec as P

EPSILON = 1e-05
LOGIT_CEILING = 30.0
RECIPROCAL_HEAT = 1.0 / 0.7


def passed_along(array, axis, by):
    size = lax.axis_size(axis)
    pairs = [(i, i + by) for i in range(size) if 0 <= i + by < size]
    return lax.ppermute(array, axis, pairs)


def normalize(values, gain):
    widened = values.astype(jnp.float32)
    scale = lax.rsqrt(jnp.mean(widened * widened, -1, keepdims=True) + EPSILON)
    return widened * scale * gain


def apply_layer(state, gain, down, upward):
    normed = normalize(state, gain).astype(jnp.bfloat16)
    latent = jax.nn.silu(jnp.dot(normed, down, preferred_element_type=jnp.float32)).astype(
        jnp.bfloat16
    )
    branch_path = jnp.dot(latent, upward, preferred_element_type=jnp.float32)
    return (state.astype(jnp.float32) + branch_path).astype(jnp.bfloat16)


def per_device(
    inputs, layer_gain, layer_down, layer_up, exit_norm_gain, head_weight, targets, exit_section
):
    section_index = lax.axis_index("section")
    section_count = lax.axis_size("section")
    micro_count = inputs.shape[0]
    mb_rows = inputs.shape[1]
    width = inputs.shape[2]
    exit_count = micro_count // section_count
    order = jnp.arange(micro_count, dtype=jnp.int32)
    same = exit_section[:, None] == exit_section[None, :]
    earlier = order[:, None] > order[None, :]
    ranks = jnp.sum((same & earlier).astype(jnp.int32), 1)
    down_full, up_full = (
        lax.all_gather(layer_down[0], "dp", axis=0, tiled=True),
        lax.all_gather(layer_up[0], "dp", axis=1, tiled=True),
    )
    section_gain = layer_gain[0]
    pieces = 1
    piece_rows = mb_rows // pieces
    piece_count = micro_count * pieces

    def advance(carry, moment):
        received, kept_state = carry
        entering = lax.dynamic_index_in_dim(
            inputs, jnp.minimum(moment, piece_count - 1), 0, keepdims=False
        )
        incoming = jnp.where(section_index == 0, entering, received)
        output = apply_layer(incoming, section_gain, down_full, up_full)
        piece_index = moment - section_index
        valid = (piece_index >= 0) & (piece_index < piece_count)
        bounded_piece = jnp.clip(piece_index, 0, piece_count - 1)
        microbatch_index = bounded_piece // pieces
        half_index = bounded_piece % pieces
        planned = lax.dynamic_index_in_dim(exit_section, microbatch_index, 0, keepdims=False)
        slot_index = lax.dynamic_index_in_dim(ranks, microbatch_index, 0, keepdims=False)
        exiting = valid & (planned == section_index)
        zero_index = jnp.zeros((), jnp.int32)
        updated = lax.dynamic_update_slice(
            kept_state, output[None, None], (slot_index, half_index, zero_index, zero_index)
        )
        kept_state = jnp.where(exiting, updated, kept_state)
        received = passed_along(output, "section", 1)
        return ((received, kept_state), None)

    empty_piece = jnp.zeros((piece_rows, width), jnp.bfloat16)
    empty_kept = jnp.zeros((exit_count, pieces, piece_rows, width), jnp.bfloat16)
    ticks = piece_count + section_count - 1
    (received, kept_state), unused = lax.scan(
        advance, (empty_piece, empty_kept), jnp.arange(ticks, dtype=jnp.int32)
    )
    kept_state = kept_state.reshape(exit_count, mb_rows, width)
    exit_in = normalize(kept_state, exit_norm_gain).astype(jnp.bfloat16)
    vocab_local = head_weight.shape[1]
    token_count = targets.shape[1]
    gathered = lax.all_gather(exit_in, "dp", axis=1, tiled=True).reshape(
        exit_count * token_count, width
    )
    score_logits = jnp.dot(
        gathered,
        lax.all_gather(head_weight, "section", axis=0, tiled=True),
        preferred_element_type=jnp.float32,
    )
    slots = jnp.arange(exit_count, dtype=jnp.int32)
    chosen = (exit_section == section_index)[None, :] & (ranks[None, :] == slots[:, None])
    micro_pick = jnp.sum(jnp.where(chosen, order[None, :], 0), 1)
    target_rows = jnp.take(targets, micro_pick, axis=0).reshape(exit_count * token_count)
    vocab_start = lax.axis_index("dp") * vocab_local
    ceiling_logits = LOGIT_CEILING * jnp.tanh(score_logits * RECIPROCAL_HEAT / LOGIT_CEILING)
    exp_total = jnp.sum(jnp.exp(ceiling_logits), -1).reshape(exit_count, token_count)
    matches = (jnp.arange(vocab_local, dtype=jnp.int32) + vocab_start)[None, :] == target_rows[
        :, None
    ]
    picked = jnp.sum(jnp.where(matches, ceiling_logits, 0.0), -1).reshape(exit_count, token_count)
    summed_total, summed_picked = lax.psum((exp_total, picked), "dp")
    row_start = lax.axis_index("dp") * mb_rows
    summed_total = lax.dynamic_slice_in_dim(summed_total, row_start, mb_rows, 1)
    summed_picked = lax.dynamic_slice_in_dim(summed_picked, row_start, mb_rows, 1)
    return (jnp.log(summed_total) - summed_picked)[None, :, :]


def solution(mesh):
    placed = (
        P(None, "dp", None),
        P("section", None),
        P("section", "dp", None),
        P("section", None, "dp"),
        P(),
        P("section", "dp"),
        P(),
        P(),
    )
    return jax.shard_map(
        per_device, mesh=mesh, in_specs=placed, out_specs=P("section", None, "dp"), check_vma=False
    )
```

profile of v0, /device:TPU:2, one launch (start us, length us, event | category | flops | bytes accessed | tf_op | source)
XLA Modules:
  0.0 1349.5 jit_solution(10418231759101149188)
XLA Ops:
  9.0 63.4 %all-gather.11.cloned.1.call-done = bf16[1,8192,128]{2,1,0:T(8,128)(2,1)} async-done(((bf16[1,256,128]{2,1,0:T(8,128)(2,1)}), bf16[1,8192,128]{2,1,0:T(8,128)(2,1)}) %all-gather.11.cloned.1.call-update) | async-done | bytes 2097168 | tf_op jit(solution)/shard_map/all_gather | solution.py:46
  72.3 64.7 %all-gather.13.cloned.1.call-done = bf16[1,128,8192]{2,1,0:T(8,128)(2,1)} async-done(((bf16[1,128,256]{2,1,0:T(8,128)(2,1)}), bf16[1,128,8192]{2,1,0:T(8,128)(2,1)}) %all-gather.13.cloned.1.call-update) | async-done | bytes 2097168 | tf_op jit(solution)/shard_map/all_gather | solution.py:47
  137.1 866.0 %while.14 = (s32[]{:T(128)}, bf16[4,8192]{1,0:T(4,128)(2,1)S(1)}, bf16[4,1,4,8192]{3,2,1,0:T(4,128)(2,1)S(1)}, pred[]{:T(512)}, s32[39]{0:T(128)S(1)}, /*index=5...) while((s32[]{:T(128)}, bf16[4,8192]{1,0:T(4,128)(2,1)S(1)}, ...), condition=%wide.region_3.4_spmd, body=%wide.region_1.3_spmd.sunk | while | flops 17238548 | bytes 5083059 | solution.py:80
  147.7 3.4 collective-permute-start
  161.2 3.1 fusion.43
  164.3 3.4 collective-permute-start
  180.9 3.8 collective-permute-start
  197.6 9.9 collective-permute-start
  219.9 10.3 collective-permute-start
  242.5 10.3 collective-permute-start
  265.2 10.3 collective-permute-start
  287.8 10.3 collective-permute-start
  310.5 10.3 collective-permute-start
  333.2 10.3 collective-permute-start
  355.8 10.3 collective-permute-start
  378.5 10.3 collective-permute-start
  401.1 10.3 collective-permute-start
  423.8 10.3 collective-permute-start
  446.4 10.3 collective-permute-start
  469.1 10.3 collective-permute-start
  491.7 10.3 collective-permute-start
  514.4 10.3 collective-permute-start
  537.1 10.3 collective-permute-start
  559.7 10.6 collective-permute-start
  582.7 10.4 collective-permute-start
  605.5 10.4 collective-permute-start
  628.3 10.3 collective-permute-start
  651.0 10.4 collective-permute-start
  673.8 10.3 collective-permute-start
  696.4 10.3 collective-permute-start
  719.1 10.3 collective-permute-start
  741.7 10.3 collective-permute-start
  764.4 10.3 collective-permute-start
  787.0 10.3 collective-permute-start
  809.7 10.3 collective-permute-start
  832.3 10.3 collective-permute-start
  855.0 10.3 collective-permute-start
  877.7 10.3 collective-permute-start
  900.3 10.3 collective-permute-start
  923.0 10.3 collective-permute-start
  945.6 10.3 collective-permute-start
  968.3 10.3 collective-permute-start
  990.9 10.3 collective-permute-start
  1005.9 84.9 %all-gather.7.cloned.1.call-done = bf16[4,128,8192]{2,0,1:T(4,128)(2,1)} async-done(((bf16[4,4,8192]{2,0,1:T(4,128)(2,1)}), bf16[4,128,8192]{2,0,1:T(4,128)(2,1)}) %all-gather.7.cloned.1.call-update) | async-done | bytes 8388624 | tf_op jit(solution)/shard_map/all_gather | solution.py:87
  1090.8 11.2 copy.13
  1102.0 162.4 %all-gather.9.cloned.1.call-done = bf16[8192,512]{1,0:T(8,128)(2,1)} async-done(((bf16[1024,512]{1,0:T(8,128)(2,1)}), bf16[8192,512]{1,0:T(8,128)(2,1)}) %all-gather.9.cloned.1.call-update) | async-done | bytes 8388624 | tf_op jit(solution)/shard_map/all_gather | solution.py:92
  1264.4 10.5 exponential_reduce_fusion
  1274.9 67.4 %all-reduce = (f32[4,128]{1,0:T(4,128)S(1)}, f32[4,128]{1,0:T(4,128)S(1)}) all-reduce(f32[4,128]{1,0:T(4,128)S(1)} %bitcast.65, f32[4,128]{1,0:T(4,128)S(1)} %bitcast.64), channel_id=1, replica_groups=mesh['section'=8,'dp'=32] {'dp'}, use_global_device_ids=true, to_apply=%region_9.10 | all-reduce | flops 1024 | bytes 8192 | tf_op jit(solution)/shard_map/psum | solution.py:106
  (302 shorter events, 339.7 us)
Async XLA Ops:
  6.5 998.7 %copy-start = (s32[32,128]{1,0:T(8,128)S(1)}, s32[32,128]{1,0:T(8,128)}, u32[]{:S(2)}) copy-start(s32[32,128]{1,0:T(8,128)} %param.16) | copy-start | bytes 49156
  6.5 65.8 %all-gather.11.cloned.1.call-start = ((), (), s32[]{:S(2)}) async-start(), calls=%async_computation.2 | async-start | bytes 2162688 | tf_op jit(solution)/shard_map/all_gather | solution.py:46
  7.3 129.8 %all-gather.13.cloned.1.call-start = ((), (), s32[]{:S(2)}) async-start(), calls=%async_computation.3 | async-start | bytes 2162688 | tf_op jit(solution)/shard_map/all_gather | solution.py:47
  8.0 1082.8 %all-gather.7.cloned.1.call-start = ((), (), s32[]{:S(2)}) async-start(), calls=%async_computation | async-start | bytes 8650752 | tf_op jit(solution)/shard_map/all_gather | solution.py:87
  137.1 866.4 %copy-start.1 = (f32[8192]{0:T(1024)S(1)}, f32[8192]{0:T(1024)}, u32[]{:S(2)}) copy-start(f32[8192]{0:T(1024)} %param.14) | copy-start | bytes 98308
  147.7 6.2 collective-permute-start
  164.3 6.2 collective-permute-start
  180.9 6.2 collective-permute-start
  197.6 11.8 collective-permute-start
  219.9 12.2 collective-permute-start
  242.5 12.2 collective-permute-start
  265.2 12.2 collective-permute-start
  287.8 12.2 collective-permute-start
  310.5 12.2 collective-permute-start
  333.2 12.2 collective-permute-start
  355.8 12.2 collective-permute-start
  378.5 12.2 collective-permute-start
  401.1 12.2 collective-permute-start
  423.8 12.2 collective-permute-start
  446.4 12.2 collective-permute-start
  469.1 12.2 collective-permute-start
  491.7 12.2 collective-permute-start
  514.4 12.2 collective-permute-start
  537.1 12.2 collective-permute-start
  559.7 12.5 collective-permute-start
  582.7 12.3 collective-permute-start
  605.5 12.3 collective-permute-start
  628.3 12.2 collective-permute-start
  651.0 12.3 collective-permute-start
  673.8 12.2 collective-permute-start
  696.4 12.2 collective-permute-start
  719.1 12.2 collective-permute-start
  741.7 12.2 collective-permute-start
  764.4 12.2 collective-permute-start
  787.0 12.2 collective-permute-start
  809.7 12.2 collective-permute-start
  832.3 12.2 collective-permute-start
  855.0 12.2 collective-permute-start
  877.7 12.2 collective-permute-start
  900.3 12.2 collective-permute-start
  923.0 12.2 collective-permute-start
  945.6 12.2 collective-permute-start
  968.3 12.2 collective-permute-start
  990.9 12.2 collective-permute-start
  1003.1 2.0 copy-start.2
  1004.5 259.9 %all-gather.9.cloned.1.call-start = ((), (), s32[]{:S(2)}) async-start(), calls=%async_computation.1 | async-start | bytes 9437184 | tf_op jit(solution)/shard_map/all_gather | solution.py:92
Sparse Core Ops, SparseCore 0:
  9.2 63.0 all-gather.10
  74.1 62.8 all-gather.12
  1004.6 86.1 all-gather.6
  1093.3 171.0 all-gather.8
where the time goes:
time: 1360 us; the launch traced here: 1350 us
  waiting for transfers between devices  453 us (33%)
  starting transfers between devices  381 us (28%)
  loops' own time  148 us (11%)
  matrix products  132 us (10%)
  local copies, waits for them, and re-layouts  111 us (8%)
  blocking collectives  67.4 us (5%)
  other arithmetic  43.5 us (3%)
    ppermute x39, starting transfers between devices, passed_along(): return lax.ppermute(array, axis, pairs)  381 us
    all_gather x1, waiting for transfers between devices, per_device(): lax.all_gather(head_weight, 'section', axis=0, tiled=True)  162 us
    another operation x1, loops' own time, per_device(): lax.scan(advance, (empty_piece, empty_kept), jnp.arange(ticks, dtype=jnp....  148 us
    dot_general x39, matrix products, apply_layer(): branch_path = jnp.dot(latent, upward, preferred_element_type=jnp.float32)  121 us
    all_gather x1, waiting for transfers between devices, per_device(): lax.all_gather(exit_in, 'dp', axis=1, tiled=True)  84.9 us
    ppermute x39, waiting for transfers between devices, passed_along(): return lax.ppermute(array, axis, pairs)  75.6 us
    psum x1, blocking collectives, per_device(): summed_total, summed_picked = lax.psum((exp_total, picked), 'dp')  67.4 us
    all_gather x1, waiting for transfers between devices, per_device(): lax.all_gather(layer_up[0], 'dp', axis=1, tiled=True)  64.7 us
  transfers between devices with their start and end apart: 43, of which 43 were waited for; matrix products, arithmetic and copies ran while one was open for 1% of the time, Pallas kernels for 0%

commit v1 on v0

v1 whole, which is shorter than its diff:
```python
import jax
import jax.numpy as jnp
from jax import lax
from jax.experimental import pallas as pl
from jax.experimental.pallas import tpu as pltpu
from jax.sharding import Mesh, PartitionSpec as P

EPSILON = 1e-05
LOGIT_CEILING = 30.0
RECIPROCAL_HEAT = 1.0 / 0.7
INTERPRET = False

SECTION = ("zhi", "x")
DP = ("zlo", "y", "core")
PLANE = ("zlo", "y")


def spread(block, axis):
    size = lax.axis_size(axis)
    copies = jnp.broadcast_to(block[None], (size, *block.shape))
    return lax.all_to_all(copies, axis, 0, 0, tiled=True)


def swapped(block):
    return lax.ppermute(block, "core", [(0, 1), (1, 0)])


def both_cores(block, axis):
    other = swapped(block)
    first = lax.axis_index("core") == 0
    low = jnp.where(first, block, other)
    high = jnp.where(first, other, block)
    return jnp.stack([low, high]) if axis is None else jnp.concatenate([low, high], axis)


def chain_kernel(exit_ref, products_ref, gram_ref, square_ref, latent_ref, scale_ref):
    layers, _, twice = products_ref.shape
    rank = twice // 2
    width = exit_ref[1].astype(jnp.float32)
    square = square_ref[...]
    for layer in range(layers):
        here = slice(layer * rank, (layer + 1) * rank)
        before = slice(0, layer * rank)
        entering = products_ref[layer, :, :rank]
        cross = products_ref[layer, :, rank:]
        if layer > 0:
            earlier = latent_ref[:, before]
            entering += jnp.dot(earlier, gram_ref[before, here], preferred_element_type=jnp.float32)
            cross += lax.dot_general(
                earlier,
                gram_ref[here, before],
                (((1,), (1,)), ((), ())),
                preferred_element_type=jnp.float32,
            )
        value = entering * lax.rsqrt(square / width + EPSILON)
        latent = (value / (1.0 + jnp.exp(-value))).astype(jnp.bfloat16)
        latent = jnp.where(layer <= exit_ref[0], latent, jnp.zeros_like(latent))
        latent_ref[:, here] = latent
        own = jnp.dot(latent, gram_ref[here, here], preferred_element_type=jnp.float32)
        grown = latent.astype(jnp.float32) * (2.0 * cross + own)
        square = jnp.maximum(square + jnp.sum(grown, -1, keepdims=True), 0.0)
    scale_ref[...] = lax.rsqrt(square / width + EPSILON)


def run_chain(numbers, products, gram, square):
    layers, rows, twice = products.shape
    whole = pl.BlockSpec(memory_space=pltpu.VMEM)
    return pl.pallas_call(
        chain_kernel,
        out_shape=(
            jax.ShapeDtypeStruct((rows, layers * twice // 2), jnp.bfloat16),
            jax.ShapeDtypeStruct((rows, 1), jnp.float32),
        ),
        in_specs=[pl.BlockSpec(memory_space=pltpu.SMEM), whole, whole, whole],
        out_specs=(whole, whole),
        compiler_params=pltpu.CompilerParams(vmem_limit_bytes=16 * 2**20),
        interpret=INTERPRET,
    )(numbers, products, gram, square)


def per_device(
    inputs, layer_gain, layer_down, layer_up, exit_norm_gain, head_weight, targets, exit_section
):
    f32, bf16 = jnp.float32, jnp.bfloat16
    section = lax.axis_index(SECTION)
    place = lax.axis_index(DP)
    micro, tokens, width = inputs.shape
    sections = lax.axis_size(SECTION)
    plane = lax.axis_size(PLANE)
    rank = layer_up.shape[1]
    own_rank = rank // lax.axis_size(DP)
    exits = micro // sections
    rows = exits * tokens
    head_rows, head_columns = head_weight.shape

    order = jnp.arange(micro, dtype=jnp.int32)
    same = exit_section[:, None] == exit_section[None, :]
    ranks = jnp.sum((same & (order[:, None] > order[None, :])).astype(jnp.int32), 1)
    slot = exit_section * exits + ranks
    chosen = jnp.sum(jnp.where(slot[None, :] == order[:, None], order[None, :], 0), 1)

    down = layer_down[0]
    up = layer_up[0]
    features = down.shape[0]
    gain = lax.dynamic_slice_in_dim(layer_gain[0], place * features, features, 0)
    scaled_down = (down.astype(f32) * gain[:, None]).astype(bf16)
    sent = up.reshape(2, 4, 4, own_rank, features).transpose(2, 1, 0, 3, 4)
    sent = sent.reshape(-1, own_rank, features)
    came = lax.all_to_all(sent, DP, 0, 0, tiled=True)
    up_rows = came.transpose(1, 0, 2).reshape(own_rank, width)
    up_rows = spread(up_rows, SECTION)
    pair = jnp.concatenate([scaled_down, up.T], 1)
    gathered = both_cores(spread(spread(pair, "zlo"), "y"), None)
    maps = gathered.transpose(2, 1, 0, 3, 4).reshape(width, 2 * rank)

    wide = inputs.astype(f32)
    squares = jnp.sum(wide * wide, -1)
    flat = jnp.concatenate(
        [inputs.reshape(micro * tokens, width), up_rows.reshape(sections * own_rank, width)], 0
    )
    products = jnp.dot(flat, maps, preferred_element_type=f32)
    state_part = jnp.take(products[: micro * tokens].reshape(micro, tokens, -1), chosen, axis=0)
    state_part = state_part.reshape(sections, rows, 2, rank).transpose(0, 2, 1, 3)
    gram_part = products[micro * tokens :].reshape(sections, own_rank, 2 * rank)
    ahead = (jnp.arange(sections, dtype=jnp.int32) < section)[:, None, None]
    gram_part = jnp.where(ahead, gram_part[..., :rank], gram_part[..., rank:])
    gram_part = gram_part.reshape(sections * own_rank, rank)
    outgoing = jnp.concatenate(
        [
            state_part.reshape(sections, 2 * rows, rank),
            jnp.broadcast_to(gram_part[None], (sections, *gram_part.shape)),
        ],
        1,
    )
    incoming = lax.all_to_all(outgoing, SECTION, 0, 0, tiled=True)
    own_products = incoming[:, : 2 * rows].reshape(sections, 2, rows, rank)
    own_products = own_products.transpose(0, 2, 1, 3).reshape(sections, rows, 2 * rank)
    gram_rows = incoming[:, 2 * rows :].transpose(1, 0, 2).astype(bf16)
    gram_rows = gram_rows.reshape(sections, own_rank, sections * rank)
    gram = both_cores(spread(spread(gram_rows, "zlo"), "y"), None)
    gram = gram.transpose(3, 0, 1, 2, 4, 5).reshape(sections * rank, sections * rank)
    own_micro = lax.dynamic_slice_in_dim(chosen, section * exits, exits, 0)
    own_square = jnp.take(squares, own_micro, axis=0).reshape(rows, 1)
    numbers = jnp.stack([section.astype(jnp.int32), jnp.int32(width)])
    latent, scale = run_chain(numbers, own_products, gram, own_square)

    head_gain = lax.dynamic_slice_in_dim(exit_norm_gain, section * head_rows, head_rows, 0)
    scaled_head = (head_weight.astype(f32) * head_gain[:, None]).astype(bf16)
    head = both_cores(scaled_head, 1)
    state_slice = lax.dynamic_slice_in_dim(inputs, section * head_rows, head_rows, 2)
    state_slice = jnp.take(state_slice, chosen, axis=0).reshape(sections, rows, head_rows)
    up_slice = lax.dynamic_slice_in_dim(up_rows, section * head_rows, head_rows, 2)
    left = jnp.concatenate([state_slice, up_slice], 1)
    left = spread(spread(left, "zlo"), "y")
    left = left.transpose(2, 1, 0, 3, 4)
    each = rows + own_rank
    partial = jnp.dot(
        left.reshape(sections * plane * each, head_rows), head, preferred_element_type=f32
    ).astype(bf16)
    partial = partial.reshape(2, 4, plane * each, 2 * head_columns)
    partial = lax.all_to_all(partial, "x", 1, 1, tiled=True)
    partial = jnp.sum(partial.astype(f32), 1).astype(bf16)
    partial = lax.all_to_all(partial, "zhi", 0, 0, tiled=True)
    total = jnp.sum(partial.astype(f32), 0).reshape(plane, each, 2 * head_columns)
    base = total[:, :rows].reshape(plane * rows, 2 * head_columns)
    correction = total[:, rows:].reshape(4, 4, own_rank, 2 * head_columns).astype(bf16)
    correction = correction.transpose(1, 0, 2, 3).reshape(-1, 2 * head_columns)
    correction = both_cores(spread(spread(correction, "zhi"), "x"), None)
    correction = correction.transpose(2, 1, 0, 3, 4).reshape(sections * rank, 2 * head_columns)

    high = lax.reduce_precision(scale, 8, 7)
    middle = lax.reduce_precision(scale - high, 8, 7)
    low = scale - high - middle
    parts = jnp.concatenate([high, middle, low], 1).astype(bf16)
    parts = jnp.pad(parts, ((0, 0), (0, 125)))
    latents = spread(jnp.concatenate([latent, parts], 1), PLANE)
    latents = latents.reshape(plane * rows, -1)
    scales = jnp.sum(latents[:, sections * rank :].astype(f32), 1, keepdims=True)
    logits = scales * (
        base + jnp.dot(latents[:, : sections * rank], correction, preferred_element_type=f32)
    )
    capped = LOGIT_CEILING * jnp.tanh(logits * RECIPROCAL_HEAT / LOGIT_CEILING)
    exp_total = jnp.sum(jnp.exp(capped), -1)
    wanted = jnp.take(targets, own_micro, axis=0).reshape(exits, plane, 2, tokens)
    wanted = lax.dynamic_index_in_dim(wanted, lax.axis_index("core"), 2, keepdims=False)
    wanted = wanted.transpose(1, 0, 2).reshape(plane * rows)
    start = lax.axis_index(PLANE) * (2 * head_columns)
    columns = jnp.arange(2 * head_columns, dtype=jnp.int32) + start
    picked = jnp.sum(jnp.where(columns[None, :] == wanted[:, None], capped, 0.0), -1)
    sums = jnp.stack([exp_total.reshape(plane, rows), picked.reshape(plane, rows)], 1)
    sums = jnp.sum(lax.all_to_all(sums, PLANE, 0, 0, tiled=True), 0)
    return (jnp.log(sums[0]) - sums[1]).reshape(1, exits, tokens)


def solution(mesh):
    devices = mesh.devices.reshape(2, 4, 4, 4, 2)
    split = Mesh(devices, SECTION + DP)
    placed = (
        P(None, DP, None),
        P(SECTION, None),
        P(SECTION, DP, None),
        P(SECTION, None, DP),
        P(),
        P(SECTION, DP),
        P(),
        P(),
    )
    return jax.shard_map(
        per_device, mesh=split, in_specs=placed, out_specs=P(SECTION, None, DP), check_vma=False
    )
```

time: 1360 us -> 425 us (0.31)
  starting transfers between devices: 381 us -> 62.1 us
  waiting for transfers between devices: 453 us -> 199 us
  loops' own time: 148 us -> 0 us
  matrix products: 132 us -> 11.4 us
  local copies, waits for them, and re-layouts: 111 us -> 54.8 us
  other arithmetic: 43.5 us -> 16.8 us
    ppermute x39 -> x4, starting transfers between devices: 381 us -> 0.28 us  [swapped(): return lax.ppermute(block, 'core', [(0, 1), (1, 0)])]
    all_gather x4 -> x0, waiting for transfers between devices: 375 us -> none  [the longest x1 162 us: per_device(): lax.all_gather(head_weight, 'section', axis=0, tiled=True)]
    all_to_all x0 -> x11, waiting for transfers between devices: none -> 196 us  [the longest x8 112 us: spread(): return lax.all_to_all(copies, axis, 0, 0, tiled=True)]
    another operation x1 -> x0, loops' own time: 148 us -> none  [per_device(): lax.scan(advance, (empty_piece, empty_kept), jnp.arange(ticks, dtype=jnp....]
    dot_general x40 -> x3, matrix products: 132 us -> 11.4 us  [the longest x1 8.44 us: per_device(): jnp.dot(left.reshape(sections * plane * each, head_rows), head, preferred...]
    dynamic_slice x117 -> x5, local copies, waits for them, and re-layouts: 99.6 us -> 1.8 us  [the longest x1 1.05 us: per_device(): lax.dynamic_slice_in_dim(inputs, section * head_rows, head_rows, 2)]
    all_to_all x0 -> x4, blocking collectives: none -> 76.1 us  [the longest x2 49.6 us: spread(): return lax.all_to_all(copies, axis, 0, 0, tiled=True)]
    ppermute x39 -> x4, waiting for transfers between devices: 75.6 us -> 2.65 us  [swapped(): return lax.ppermute(block, 'core', [(0, 1), (1, 0)])]
  transfers between devices with their start and end apart: 43 -> 15, of which waited for: 43 -> 10; matrix products, arithmetic and copies ran while one was open for 1% -> 16% of each run, Pallas kernels for 0% -> 1%
where the time goes in v1:
time: 425 us; the launch traced here: 424 us
  waiting for transfers between devices  199 us (47%)
  blocking collectives  76.1 us (18%)
  starting transfers between devices  62.1 us (15%)
  local copies, waits for them, and re-layouts  54.8 us (13%)
  other arithmetic  16.8 us (4%)
  matrix products  11.4 us (3%)
    all_to_all x8, waiting for transfers between devices, spread(): return lax.all_to_all(copies, axis, 0, 0, tiled=True)  112 us
    all_to_all x1, waiting for transfers between devices, per_device(): partial = lax.all_to_all(partial, 'x', 1, 1, tiled=True)  55.7 us
    all_to_all x2, blocking collectives, spread(): return lax.all_to_all(copies, axis, 0, 0, tiled=True)  49.6 us
    all_to_all x8, starting transfers between devices, spread(): return lax.all_to_all(copies, axis, 0, 0, tiled=True)  46.8 us
    all_to_all x1, waiting for transfers between devices, per_device(): partial = lax.all_to_all(partial, 'zhi', 0, 0, tiled=True)  20.9 us
    all_to_all x1, blocking collectives, per_device(): incoming = lax.all_to_all(outgoing, SECTION, 0, 0, tiled=True)  14.1 us
    all_to_all x1, blocking collectives, per_device(): sums = jnp.sum(lax.all_to_all(sums, PLANE, 0, 0, tiled=True), 0)  12.3 us
    broadcast_in_dim x12, local copies, waits for them, and re-layouts, spread(): copies = jnp.broadcast_to(block[None], (size, *block.shape))  10.6 us
  transfers between devices with their start and end apart: 15, of which 10 were waited for; matrix products, arithmetic and copies ran while one was open for 16% of the time, Pallas kernels for 1%

profile of v1, /device:TPU:2, one launch (start us, length us, event | category | flops | bytes accessed | tf_op | source)
XLA Modules:
  0.0 423.6 jit_solution(9011619038270638223)
XLA Ops:
  2.0 20.2 %all_to_all.75 = bf16[4,256,256]{2,1,0:T(8,128)(2,1)S(1)} all-to-all(bf16[4,256,256]{2,1,0:T(8,128)(2,1)S(1)} %broadcast_in_dim.152), channel_id=1, replica_groups=mesh['zhi'=2,'x'=4,'zlo'=4,'y'=4,'core'=2] {'zlo'}, dimensions={0} | all-to-all | bytes 1048576 | tf_op jit(solution)/shard_map/all_to_all | solution.py:21
  22.4 29.5 %all_to_all.76 = bf16[4,4,256,256]{3,2,1,0:T(8,128)(2,1)S(1)} all-to-all(bf16[4,4,256,256]{3,2,1,0:T(8,128)(2,1)S(1)} %broadcast_in_dim.153), channel_id=1, replica_groups=mesh['zhi'=2,'x'=4,'zlo'=4,'y'=4,'core'=2] {'y'}, dimensions={0} | all-to-all | bytes 4194304 | tf_op jit(solution)/shard_map/all_to_all | solution.py:21
  51.9 1.5 copy.135
  54.0 4.5 %all-to-all-start = ((bf16[32,4,256]{2,1,0:T(4,128)(2,1)}), bf16[32,4,256]{2,1,0:T(4,128)(2,1)S(1)}, u32[]{:S(2)}, u32[]{:S(2)}) async-start(bf16[32,4,256]{2,1,0:T(4,128)(2,1)} %bitcast.3), calls=%async_computation | async-start | bytes 131072 | tf_op jit(solution)/shard_map/all_to_all | solution.py:109
  58.9 7.6 %all-to-all-done = bf16[32,4,256]{2,1,0:T(4,128)(2,1)S(1)} async-done(((bf16[32,4,256]{2,1,0:T(4,128)(2,1)}), bf16[32,4,256]{2,1,0:T(4,128)(2,1)S(1)}, u32[]{:S(2)}, u32[]{:S(2)}) %all-to-all-start) | async-done | bytes 65568 | tf_op jit(solution)/shard_map/all_to_all | solution.py:109
  67.4 8.8 %all-to-all-start.1 = ((bf16[8,4,8192]{2,1,0:T(4,128)(2,1)}), bf16[8,4,8192]{2,1,0:T(4,128)(2,1)S(1)}, u32[]{:S(2)}, u32[]{:S(2)}) async-start(bf16[8,4,8192]{2,1,0:T(4,128)(2,1)} %broadcast_in_dim.151), calls=%async_computation.1 | async-start | bytes 1048576 | tf_op jit(solution)/shard_map/all_to_all | solution.py:21
  76.2 1.0 constant_dynamic-slice_fusion.1
  78.4 11.4 %all-to-all-done.1 = bf16[8,4,8192]{2,1,0:T(4,128)(2,1)S(1)} async-done(((bf16[8,4,8192]{2,1,0:T(4,128)(2,1)}), bf16[8,4,8192]{2,1,0:T(4,128)(2,1)S(1)}, u32[]{:S(2)}, u32[]{:S(2)}) %all-to-all-start.1) | async-done | bytes 524320 | tf_op jit(solution)/shard_map/all_to_all | solution.py:21
  89.9 1.2 broadcast_in_dim.166
  91.2 5.5 %all-to-all-start.8 = ((bf16[4,8,20,1024]{3,1,2,0:T(8,128)(2,1)}), bf16[4,8,20,1024]{3,1,2,0:T(8,128)(2,1)S(1)}, u32[]{:S(2)}, u32[]{:S(2)}) async-start(bf16[4,8,20,1024]{3,1,2,0:T(8,128)(2,1)} %broadcast_in_dim.166), calls=%async_computation.8 | async-start | bytes 2621440 | tf_op jit(solution)/shard_map/all_to_all | solution.py:21
  96.6 4.0 reshape.165
  100.7 2.0 reshape.167
  102.7 1.9 select_bitcast_fusion.1
  105.0 1.2 copy-done.8
  108.3 19.4 %all-to-all-done.8 = bf16[4,8,20,1024]{3,1,2,0:T(8,128)(2,1)S(1)} async-done(((bf16[4,8,20,1024]{3,1,2,0:T(8,128)(2,1)}), bf16[4,8,20,1024]{3,1,2,0:T(8,128)(2,1)S(1)}, u32[]{:S(2)}, u32[]{:S(2)}) %all-to-all-start.8) | async-done | bytes 1310752 | tf_op jit(solution)/shard_map/all_to_all | solution.py:21
  127.7 14.1 %all_to_all.77 = f32[8,64,128]{2,1,0:T(8,128)} all-to-all(f32[8,64,128]{2,1,0:T(8,128)S(1)} %pad_maximum_fusion.3), channel_id=1, replica_groups=mesh['zhi'=2,'x'=4,'zlo'=4,'y'=4,'core'=2] {'zhi','x'}, dimensions={0} | all-to-all | bytes 524288 | tf_op jit(solution)/shard_map/all_to_all | solution.py:135
  141.8 3.0 broadcast_in_dim.167
  144.8 5.2 %all-to-all-start.9 = ((bf16[4,4,8,20,1024]{4,2,3,1,0:T(8,128)(2,1)}), bf16[4,4,8,20,1024]{4,2,3,1,0:T(8,128)(2,1)}, u32[]{:S(2)}, u32[]{:S(2)}) async-start(bf16[4,4,8,20,1024]{4,2,3,1,0:T(8,128)(2,1)} %broadcast_in_dim.167), calls=%async_computation.9 | async-start | bytes 10485760 | tf_op jit(solution)/shard_map/all_to_all | solution.py:21
  151.1 2.6 collective-permute-done.2
  154.4 53.8 %all-to-all-done.9 = bf16[4,4,8,20,1024]{4,2,3,1,0:T(8,128)(2,1)} async-done(((bf16[4,4,8,20,1024]{4,2,3,1,0:T(8,128)(2,1)}), bf16[4,4,8,20,1024]{4,2,3,1,0:T(8,128)(2,1)}, u32[]{:S(2)}, u32[]{:S(2)}) %all-to-all-start.9) | async-done | bytes 5242912 | tf_op jit(solution)/shard_map/all_to_all | solution.py:21
  208.9 3.6 all-to-all-start.5
  212.5 8.2 %copy.146 = bf16[8,4,4,20,1024]{4,3,2,1,0:T(8,128)(2,1)} copy(bf16[8,4,4,20,1024]{4,0,3,1,2:T(8,128)(2,1)} %bitcast.27) | data formatting | bytes 10485760 | tf_op jit(solution)/shard_map/transpose | solution.py:155
  220.7 9.0 %reshape.176 = bf16[2560,1024]{1,0:T(8,128)(2,1)} reshape(bf16[8,4,4,20,1024]{4,3,2,1,0:T(8,128)(2,1)} %copy.146) | data formatting | bytes 10485760 | tf_op jit(solution)/shard_map/reshape | solution.py:158
  229.7 8.4 %convolution_convert_fusion = bf16[2560,1024]{1,0:T(8,128)(2,1)S(1)} fusion(bf16[2560,1024]{1,0:T(8,128)(2,1)} %reshape.176, bf16[1024,512]{1,0:T(8,128)(2,1)S(1)} %get-tuple-element.20, bf16[1024,512]{1,0:T(8,128)(2,1)S(1)} %get-tuple-element.19), kind=kOutput, calls=%fused_computation.4 | convolution fusion | flops 5375524864 | bytes 12582912 | tf_op jit(solution)/shard_map/dot_general | solution.py:157
  238.1 3.4 copy.147
  241.5 6.8 %all-to-all-start.10 = ((bf16[2,4,320,1024]{3,2,0,1:T(8,128)(2,1)}), bf16[2,4,320,1024]{3,2,0,1:T(8,128)(2,1)}, u32[]{:S(2)}, u32[]{:S(2)}) async-start(bf16[2,4,320,1024]{3,2,0,1:T(8,128)(2,1)} %copy.147), calls=%async_computation.10 | async-start | bytes 10485760 | tf_op jit(solution)/shard_map/all_to_all | solution.py:161
  248.4 55.7 %all-to-all-done.10 = bf16[2,4,320,1024]{3,2,0,1:T(8,128)(2,1)} async-done(((bf16[2,4,320,1024]{3,2,0,1:T(8,128)(2,1)}), bf16[2,4,320,1024]{3,2,0,1:T(8,128)(2,1)}, u32[]{:S(2)}, u32[]{:S(2)}) %all-to-all-start.10) | async-done | bytes 5242912 | tf_op jit(solution)/shard_map/all_to_all | solution.py:161
  304.1 1.5 broadcast_in_dim.160
  305.6 3.5 all-to-all-start.6
  309.1 5.2 %reduce_sum.94 = bf16[2,320,1024]{2,1,0:T(8,128)(2,1)} reduce(bf16[2,4,320,1024]{3,2,0,1:T(8,128)(2,1)} %all-to-all-done.10, bf16[]{:T(256)} %constant.100.clone.1), dimensions={1}, to_apply=%region_4.5 | reduce | flops 1966080 | bytes 6553602 | tf_op jit(solution)/shard_map/reduce_sum | solution.py:162
  314.3 6.1 %all-to-all-done.6 = bf16[4,4,8,4,1024]{4,3,1,2,0:T(4,128)(2,1)S(1)} async-done(((bf16[4,4,8,4,1024]{4,3,1,2,0:T(4,128)(2,1)}), bf16[4,4,8,4,1024]{4,3,1,2,0:T(4,128)(2,1)S(1)}, u32[]{:S(2)}, u32[]{:S(2)}) %all-to-all-start.6) | async-done | bytes 1048608 | tf_op jit(solution)/shard_map/all_to_all | solution.py:21
  321.4 3.6 all-to-all-start.11
  325.2 1.2 multiply_reduce_fusion
  326.9 20.9 %all-to-all-done.11 = bf16[2,320,1024]{2,1,0:T(8,128)(2,1)S(1)} async-done(((bf16[2,320,1024]{2,1,0:T(8,128)(2,1)}), bf16[2,320,1024]{2,1,0:T(8,128)(2,1)S(1)}, u32[]{:S(2)}, u32[]{:S(2)}) %all-to-all-start.11) | async-done | bytes 1310752 | tf_op jit(solution)/shard_map/all_to_all | solution.py:163
  349.3 3.7 all-to-all-start.12
  353.3 8.6 %all-to-all-done.12 = bf16[2,64,1024]{2,1,0:T(8,128)(2,1)S(1)} async-done(((bf16[2,64,1024]{2,1,0:T(8,128)(2,1)}), bf16[2,64,1024]{2,1,0:T(8,128)(2,1)S(1)}, u32[]{:S(2)}, u32[]{:S(2)}) %all-to-all-start.12) | async-done | bytes 262176 | tf_op jit(solution)/shard_map/all_to_all | solution.py:21
  361.8 1.1 broadcast_in_dim.170
  363.0 4.9 %all-to-all-start.13 = ((bf16[4,2,64,1024]{3,2,1,0:T(8,128)(2,1)}), bf16[4,2,64,1024]{3,2,1,0:T(8,128)(2,1)S(1)}, u32[]{:S(2)}, u32[]{:S(2)}) async-start(bf16[4,2,64,1024]{3,2,1,0:T(8,128)(2,1)} %broadcast_in_dim.170), calls=%async_computation.13 | async-start | bytes 2097152 | tf_op jit(solution)/shard_map/all_to_all | solution.py:21
  367.9 2.1 select_bitcast_fusion.5
  370.0 1.5 maximum_bitcast_fusion
  371.5 2.2 copy.142
  373.8 2.5 reshape.174.gram_ref
  376.3 2.8 shard_map.82
  380.2 11.7 %all-to-all-start.7 = ((bf16[16,16,1152]{2,1,0:T(8,128)(2,1)}), bf16[16,16,1152]{2,1,0:T(8,128)(2,1)}, u32[]{:S(2)}, u32[]{:S(2)}) async-start(bf16[16,16,1152]{2,1,0:T(8,128)(2,1)} %broadcast_in_dim.163), calls=%async_computation.7 | async-start | bytes 1179648 | tf_op jit(solution)/shard_map/all_to_all | solution.py:21
  393.0 12.8 %all-to-all-done.7 = bf16[16,16,1152]{2,1,0:T(8,128)(2,1)} async-done(((bf16[16,16,1152]{2,1,0:T(8,128)(2,1)}), bf16[16,16,1152]{2,1,0:T(8,128)(2,1)}, u32[]{:S(2)}, u32[]{:S(2)}) %all-to-all-start.7) | async-done | bytes 589856 | tf_op jit(solution)/shard_map/all_to_all | solution.py:21
  407.2 1.0 slice-done
  408.2 2.1 exponential_reduce_fusion
  410.5 12.3 %all_to_all.78 = f32[16,2,16]{2,1,0:T(2,128)S(1)} all-to-all(f32[16,2,16]{2,1,0:T(2,128)S(1)} %pad_maximum_fusion.6), channel_id=1, replica_groups=mesh['zhi'=2,'x'=4,'zlo'=4,'y'=4,'core'=2] {'zlo','y'}, dimensions={0} | all-to-all | bytes 4096 | tf_op jit(solution)/shard_map/all_to_all | solution.py:191
  (120 shorter events, 18.1 us)
Async XLA Ops:
  0.0 1.0 copy-start
  51.9 1.5 copy-start.11
  51.9 6.7 %copy-start.13 = (s32[32]{0:T(128)S(1)}, s32[32]{0:T(128)}, u32[]{:S(2)}) copy-start(s32[32]{0:T(128)} %param.15) | copy-start | bytes 388
  53.4 49.3 %collective-permute-start = (bf16[4,4,256,256]{3,2,0,1:T(8,128)(2,1)}, bf16[4,4,256,256]{3,2,0,1:T(8,128)(2,1)}, u32[]{:S(2)}, u32[]{:S(2)}) collective-permute-start(bf16[4,4,256,256]{3,2,0,1:T(8,128)(2,1)} %copy.135), channel_id=1, source_target_pairs={{0,1},{1,0},{2,3},{3,2},{4,5},{5,4},{6,7},{7,6},{8,9},{9,8},{10,11... | collective-permute-start | bytes 6291464 | tf_op jit(solution)/shard_map/ppermute | solution.py:25
  54.0 12.4 %all-to-all-start = ((bf16[32,4,256]{2,1,0:T(4,128)(2,1)}), bf16[32,4,256]{2,1,0:T(4,128)(2,1)S(1)}, u32[]{:S(2)}, u32[]{:S(2)}) async-start(bf16[32,4,256]{2,1,0:T(4,128)(2,1)} %bitcast.3), calls=%async_computation | async-start | bytes 131072 | tf_op jit(solution)/shard_map/all_to_all | solution.py:109
  67.4 22.4 %all-to-all-start.1 = ((bf16[8,4,8192]{2,1,0:T(4,128)(2,1)}), bf16[8,4,8192]{2,1,0:T(4,128)(2,1)S(1)}, u32[]{:S(2)}, u32[]{:S(2)}) async-start(bf16[8,4,8192]{2,1,0:T(4,128)(2,1)} %broadcast_in_dim.151), calls=%async_computation.1 | async-start | bytes 1048576 | tf_op jit(solution)/shard_map/all_to_all | solution.py:21
  89.8 1.3 copy-start.7
  91.2 36.5 %all-to-all-start.8 = ((bf16[4,8,20,1024]{3,1,2,0:T(8,128)(2,1)}), bf16[4,8,20,1024]{3,1,2,0:T(8,128)(2,1)S(1)}, u32[]{:S(2)}, u32[]{:S(2)}) async-start(bf16[4,8,20,1024]{3,1,2,0:T(8,128)(2,1)} %broadcast_in_dim.166), calls=%async_computation.8 | async-start | bytes 2621440 | tf_op jit(solution)/shard_map/all_to_all | solution.py:21
  104.6 1.6 copy-start.8
  104.6 1.7 copy-start.10
  144.8 5.9 %copy-start.4 = (bf16[1024,512]{1,0:T(8,128)(2,1)S(1)}, bf16[1024,512]{1,0:T(8,128)(2,1)}, u32[]{:S(2)}) copy-start(bf16[1024,512]{1,0:T(8,128)(2,1)} %param.13) | copy-start | bytes 3145732
  144.8 63.3 %all-to-all-start.9 = ((bf16[4,4,8,20,1024]{4,2,3,1,0:T(8,128)(2,1)}), bf16[4,4,8,20,1024]{4,2,3,1,0:T(8,128)(2,1)}, u32[]{:S(2)}, u32[]{:S(2)}) async-start(bf16[4,4,8,20,1024]{4,2,3,1,0:T(8,128)(2,1)} %broadcast_in_dim.167), calls=%async_computation.9 | async-start | bytes 10485760 | tf_op jit(solution)/shard_map/all_to_all | solution.py:21
  151.0 3.3 copy-start.9
  151.0 2.7 collective-permute-start.2
  208.9 32.5 %all-to-all-start.5 = ((bf16[4,8,4,1024]{3,2,1,0:T(4,128)(2,1)}), bf16[4,8,4,1024]{3,2,1,0:T(4,128)(2,1)S(1)}, u32[]{:S(2)}, u32[]{:S(2)}) async-start(bf16[4,8,4,1024]{3,2,1,0:T(4,128)(2,1)} %broadcast_in_dim.159), calls=%async_computation.5 | async-start | bytes 524288 | tf_op jit(solution)/shard_map/all_to_all | solution.py:21
  241.5 62.7 %all-to-all-start.10 = ((bf16[2,4,320,1024]{3,2,0,1:T(8,128)(2,1)}), bf16[2,4,320,1024]{3,2,0,1:T(8,128)(2,1)}, u32[]{:S(2)}, u32[]{:S(2)}) async-start(bf16[2,4,320,1024]{3,2,0,1:T(8,128)(2,1)} %copy.147), calls=%async_computation.10 | async-start | bytes 10485760 | tf_op jit(solution)/shard_map/all_to_all | solution.py:161
  305.6 14.8 %all-to-all-start.6 = ((bf16[4,4,8,4,1024]{4,3,1,2,0:T(4,128)(2,1)}), bf16[4,4,8,4,1024]{4,3,1,2,0:T(4,128)(2,1)S(1)}, u32[]{:S(2)}, u32[]{:S(2)}) async-start(bf16[4,4,8,4,1024]{4,3,1,2,0:T(4,128)(2,1)} %broadcast_in_dim.160), calls=%async_computation.6 | async-start | bytes 2097152 | tf_op jit(solution)/shard_map/all_to_all | solution.py:21
  314.3 10.9 %copy-start.2 = (bf16[32,4,8192]{2,1,0:T(4,128)(2,1)S(1)}, bf16[32,4,8192]{2,1,0:T(4,128)(2,1)}, u32[]{:S(2)}) copy-start(bf16[32,4,8192]{2,1,0:T(4,128)(2,1)} %param.8) | copy-start | bytes 6291460
  320.4 1.0 copy-start.5
  321.4 26.5 %all-to-all-start.11 = ((bf16[2,320,1024]{2,1,0:T(8,128)(2,1)}), bf16[2,320,1024]{2,1,0:T(8,128)(2,1)S(1)}, u32[]{:S(2)}, u32[]{:S(2)}) async-start(bf16[2,320,1024]{2,1,0:T(8,128)(2,1)} %reduce_sum.94), calls=%async_computation.11 | async-start | bytes 2621440 | tf_op jit(solution)/shard_map/all_to_all | solution.py:163
  325.0 42.9 %collective-permute-start.1 = (bf16[4,4,8,4,1024]{4,3,1,2,0:T(4,128)(2,1)}, bf16[4,4,8,4,1024]{4,3,1,2,0:T(4,128)(2,1)}, u32[]{:S(2)}, u32[]{:S(2)}) collective-permute-start(bf16[4,4,8,4,1024]{4,3,1,2,0:T(4,128)(2,1)} %copy-done.5), channel_id=1, source_target_pairs={{0,1},{1,0},{2,3},{3,2},{4,5},{5,4},{6,7},{7,6},{8,9},{9,8},{10,11... | collective-permute-start | bytes 3145736 | tf_op jit(solution)/shard_map/ppermute | solution.py:25
  348.1 5.1 %slice-start.1 = ((f32[8,64,128]{2,1,0:T(8,128)}), f32[8,32,128]{2,1,0:T(8,128)S(1)}, s32[]{:S(2)}) async-start(f32[8,64,128]{2,1,0:T(8,128)} %all_to_all.77), calls=%async_computation.16 | async-start | bytes 262144 | tf_op jit(solution)/shard_map/slice | solution.py:136
  348.3 14.7 %copy-start.3 = (f32[16,20,1024]{2,1,0:T(8,128)}, f32[16,20,1024]{2,1,0:T(8,128)S(1)}, u32[]{:S(2)}) copy-start(f32[16,20,1024]{2,1,0:T(8,128)S(1)} %reshape.178) | copy-start | bytes 3932164
  349.3 12.5 %all-to-all-start.12 = ((bf16[2,64,1024]{2,1,0:T(8,128)(2,1)}), bf16[2,64,1024]{2,1,0:T(8,128)(2,1)S(1)}, u32[]{:S(2)}, u32[]{:S(2)}) async-start(bf16[2,64,1024]{2,1,0:T(8,128)(2,1)} %broadcast_in_dim.169), calls=%async_computation.12 | async-start | bytes 524288 | tf_op jit(solution)/shard_map/all_to_all | solution.py:21
  353.0 14.9 %copy-start.6 = (bf16[4,4,8,4,1024]{4,3,1,2,0:T(4,128)(2,1)S(1)}, bf16[4,4,8,4,1024]{4,3,1,2,0:T(4,128)(2,1)}, u32[]{:S(2)}) copy-start(bf16[4,4,8,4,1024]{4,3,1,2,0:T(4,128)(2,1)} %copy-done.5) | copy-start | bytes 3145732
  363.0 16.3 %all-to-all-start.13 = ((bf16[4,2,64,1024]{3,2,1,0:T(8,128)(2,1)}), bf16[4,2,64,1024]{3,2,1,0:T(8,128)(2,1)S(1)}, u32[]{:S(2)}, u32[]{:S(2)}) async-start(bf16[4,2,64,1024]{3,2,1,0:T(8,128)(2,1)} %broadcast_in_dim.170), calls=%async_computation.13 | async-start | bytes 2097152 | tf_op jit(solution)/shard_map/all_to_all | solution.py:21
  379.1 12.9 %copy-start.12 = (s32[32,128]{1,0:T(8,128)S(1)}, s32[32,128]{1,0:T(8,128)}, u32[]{:S(2)}) copy-start(s32[32,128]{1,0:T(8,128)} %param.14) | copy-start | bytes 49156
  380.2 25.7 %all-to-all-start.7 = ((bf16[16,16,1152]{2,1,0:T(8,128)(2,1)}), bf16[16,16,1152]{2,1,0:T(8,128)(2,1)}, u32[]{:S(2)}, u32[]{:S(2)}) async-start(bf16[16,16,1152]{2,1,0:T(8,128)(2,1)} %broadcast_in_dim.163), calls=%async_computation.7 | async-start | bytes 1179648 | tf_op jit(solution)/shard_map/all_to_all | solution.py:21
  392.0 14.9 %collective-permute-start.3 = (bf16[4,2,64,1024]{3,2,0,1:T(8,128)(2,1)S(1)}, bf16[4,2,64,1024]{3,2,0,1:T(8,128)(2,1)S(1)}, u32[]{:S(2)}, u32[]{:S(2)}) collective-permute-start(bf16[4,2,64,1024]{3,2,0,1:T(8,128)(2,1)S(1)} %copy.150), channel_id=1, source_target_pairs={{0,1},{1,0},{2,3},{3,2},{4,5},{5,4},{6,7},{7,6},{8,9},{9,8},{10,11... | collective-permute-start | bytes 3145736 | tf_op jit(solution)/shard_map/ppermute | solution.py:25
  407.0 1.2 slice-start
  407.2 16.4 %copy-start.1 = (f32[1,8192]{1,0:T(1,128)S(1)}, f32[1,8192]{1,0:T(1,128)}, u32[]{:S(2)}) copy-start(f32[1,8192]{1,0:T(1,128)} %param.9) | copy-start | bytes 98308
